TPU v7x, 256 devices: a whole 4x4x8 slice. The times are simulated.
256 devices in a mesh: row: 32 (over y, z), col: 8 (over x, core).
Axes of the slice: x: 4, y: 4, z: 8, core: 2. Of those that a mesh axis runs over, the one named last changes fastest.
Arguments:
- embeddings: bfloat16 [4096, 1024], P(('row', 'col')), may hold values from -20 to 20
- group_ids: int32 [4096], P(('row', 'col')), may hold values from 0 to 1023, as said below
Outputs:
- loss: float32 [], replicated
- grad: bfloat16 [4096, 1024], P(('row', 'col'))
Inputs may be any that keep to these rules, and one draw needn't show every extreme that they name: `group_ids`: every group id is held by exactly 4 rows, spread over the batch.
All inputs are finite; a program needn't handle non-finite values.
Results may differ from a plain program's by a relative error of at most 0.0045.
Values may be sent and summed in bfloat16 or wider, within the bound.
A program may use at most 64 MiB of HBM per device.

v0:
```python
import jax
import jax.numpy as jnp
from jax import lax
from jax.sharding import Mesh
from jax.sharding import PartitionSpec as P

ROW = ("row_0", "row_1")
COL = ("col_0", "col_1")
ROW_COL = ("row_0", "row_1", "col_0", "col_1")


def joined_along(parts, dim):
    parts = jnp.moveaxis(parts, 0, dim)
    dims = parts.shape
    return parts.reshape(*dims[:dim], dims[dim] * dims[dim + 1], *dims[dim + 2 :])


def stacked_from(x, axes, turns):
    parts = x
    for k in turns:
        parts = lax.all_gather(parts, axes[k])
    done = turns[::-1]
    back = [done.index(k) for k in range(len(axes))]
    parts = parts.transpose(*back, *range(len(axes), parts.ndim))
    return parts.reshape(-1, *x.shape)


def whole_of(x, axes, turns, dim):
    return joined_along(stacked_from(x, axes, turns), dim)


def sent_to_all(x, axis):
    copies = jnp.broadcast_to(x, (lax.axis_size(axis), *x.shape))
    return lax.all_to_all(copies, axis, split_axis=0, concat_axis=0, tiled=True)


def gathered_copies(x, axis, dim):
    parts = sent_to_all(x, axis)
    return joined_along(parts, dim)


def all_in_one(x, axis):
    leaves = jax.tree.leaves(x)
    turns = sorted(range(len(leaves)), key=lambda k: -leaves[k].size)
    width = (1, *leaves[turns[0]].shape)[-1]
    lines = [
        jnp.pad(leaves[k].reshape(-1), (0, -leaves[k].size % width)).reshape(-1, width)
        for k in turns
    ]
    both, at, found = (sent_to_all(jnp.concatenate(lines), axis), 0, {})
    for k, line in zip(turns, lines):
        share = both[:, at : at + len(line)].reshape(len(both), -1)
        found[k] = share[:, : leaves[k].size].reshape(-1, *leaves[k].shape)
        at += len(line)
    numbers = iter(range(len(leaves)))
    return jax.tree.map(lambda _: found[next(numbers)], x)


def combined_pairwise(pieces, combine):
    while len(jax.tree.leaves(pieces)[0]) > 1:
        pieces = jax.vmap(combine)(
            *(jax.tree.map(lambda part: part[side::2], pieces) for side in (0, 1))
        )
    return jax.tree.map(lambda part: part[0], pieces)


def merged(x, axis, combine):
    pieces = all_in_one(x, axis)
    return combined_pairwise(pieces, combine)


def one_axis_at_a_time(x, axes):
    for axis in axes:
        x = lax.psum(x, axis)
    return x


def rows_first(arrays, axis, dims):
    turned = [jnp.moveaxis(a, dim, 0) for a, dim in zip(arrays, dims)]
    widths = [t[0].size for t in turned]
    both = jnp.concatenate([t.reshape(-1, w) for t, w in zip(turned, widths)], axis=1)
    result = lax.all_gather(both, axis, axis=0, tiled=True)
    parts = jnp.split(result, [sum(widths[:k]) for k in range(1, len(widths))], axis=1)
    return tuple(
        (
            jnp.moveaxis(b.reshape(-1, *t.shape[1:]), 0, dim)
            for b, t, dim in zip(parts, turned, dims)
        )
    )


def split_up(x, dim, size):
    before, after = (x.shape[:dim], x.shape[dim + 1 :])
    return jnp.moveaxis(x.reshape(*before, size, -1, *after), dim, 0)


def sent_and_summed(x, axis, dim):
    parts = split_up(x, dim, lax.axis_size(axis))
    arrived = lax.all_to_all(parts, axis, split_axis=0, concat_axis=0, tiled=True)
    return arrived.sum(axis=0)


def combine_stats(first, second):
    peak = jnp.maximum(first[0], second[0])
    total = first[1] * jnp.exp(first[0] - peak) + second[1] * jnp.exp(second[0] - peak)
    return (peak, total, first[2] + second[2], first[3] + second[3])


def on_device(embeddings, group_ids):
    row_count = lax.axis_size(ROW)
    col_count = lax.axis_size(COL)
    row_index = lax.axis_index(ROW)
    col_index = lax.axis_index(COL)
    rows = embeddings.shape[0]
    width = embeddings.shape[1]
    scale = 1.0 / jnp.sqrt(jnp.float32(width))
    whole = rows * row_count * col_count
    queries, query_groups = (
        whole_of(embeddings, ("col_0", "col_1"), (0, 1), 0),
        whole_of(group_ids, ("col_0", "col_1"), (0, 1), 0),
    )
    keys, key_groups = (gathered_copies(embeddings, ROW, 0), gathered_copies(group_ids, ROW, 0))
    query_len = rows * col_count
    key_len = rows * row_count
    query_pos = row_index * query_len + jnp.arange(query_len, dtype=jnp.int32)
    key_local = jnp.arange(key_len, dtype=jnp.int32)
    key_pos = (key_local // rows * col_count + col_index) * rows + key_local % rows
    scores = (
        lax.dot_general(queries, keys, (((1,), (1,)), ((), ())), preferred_element_type=jnp.float32)
        * scale
    )
    selfs = query_pos[:, None] == key_pos[None, :]
    positive = jnp.logical_and(query_groups[:, None] == key_groups[None, :], jnp.logical_not(selfs))
    masked = jnp.where(selfs, jnp.float32(-1e30), scores)
    peak = jnp.max(masked, axis=1)
    total = jnp.sum(jnp.exp(masked - peak[:, None]), axis=1)
    possum = jnp.sum(jnp.where(positive, scores, jnp.float32(0.0)), axis=1)
    count = jnp.sum(positive.astype(jnp.float32), axis=1)
    peak, total, possum, count = merged((peak, total, possum, count), COL, combine_stats)
    lse = peak + jnp.log(total)
    inverse = 1.0 / count
    row_loss = lse - possum * inverse
    own_start = col_index * rows
    own_loss = lax.dynamic_slice_in_dim(row_loss, own_start, rows, 0)
    loss = one_axis_at_a_time(jnp.sum(own_loss), ROW_COL) / whole
    weight = (
        jnp.exp(masked - lse[:, None]) - jnp.where(positive, inverse[:, None], jnp.float32(0.0))
    ) / whole
    weight = weight.astype(jnp.bfloat16)
    own_lse = lax.dynamic_slice_in_dim(lse, own_start, rows, 0)
    own_inverse = lax.dynamic_slice_in_dim(inverse, own_start, rows, 0)
    key_lse, key_inverse = rows_first((own_lse, own_inverse), ROW, (0, 0))
    mirrored = (
        jnp.exp(masked - key_lse[None, :])
        - jnp.where(positive, key_inverse[None, :], jnp.float32(0.0))
    ) / whole
    mirrored = mirrored.astype(jnp.bfloat16)
    both_term = jnp.dot(weight, keys, preferred_element_type=jnp.float32) + jnp.dot(
        mirrored, keys, preferred_element_type=jnp.float32
    )
    grad = scale * sent_and_summed(both_term, COL, 0)
    return (loss, grad.astype(jnp.bfloat16))


def solution(mesh):
    split = Mesh(mesh.devices.reshape(4, 8, 4, 2), ("row_0", "row_1", "col_0", "col_1"))
    in_specs = (P(ROW_COL, None), P(ROW_COL))
    out_specs = (P(), P(ROW_COL, None))
    return jax.shard_map(
        on_device, mesh=split, in_specs=in_specs, out_specs=out_specs, check_vma=False
    )
```

profile of v0, /device:TPU:32, one launch (start us, length us, event | category | flops | bytes accessed | tf_op | source)
XLA Modules:
  0.0 157.8 jit_solution(6064732882702261345)
XLA Ops:
  0.6 0.0 copy-start
  0.6 0.7 broadcast_in_dim.46
  1.3 19.8 %all_to_all.21 = s32[32,1,16]{2,1,0:T(1,128)S(1)} all-to-all(s32[32,1,16]{2,1,0:T(1,128)S(1)} %broadcast_in_dim.46), channel_id=1, replica_groups=mesh['row_0'=4,'row_1'=8,'col_0'=4,'col_1'=2] {'row_0','row_1'}, dimensions={0} | all-to-all | bytes 4096 | tf_op jit(solution)/shard_map/all_to_all | solution.py:34
  21.1 0.0 copy-done
  21.1 1.1 broadcast_in_dim.45
  22.2 5.0 %all-to-all-start = ((bf16[32,16,1024]{2,1,0:T(8,128)(2,1)}), bf16[32,16,1024]{2,1,0:T(8,128)(2,1)S(1)}, u32[]{:S(2)}, u32[]{:S(2)}) async-start(bf16[32,16,1024]{2,1,0:T(8,128)(2,1)} %broadcast_in_dim.45), calls=%async_computation | async-start | bytes 2097152 | tf_op jit(solution)/shard_map/all_to_all | solution.py:34
  27.2 12.3 %all-gather = bf16[64,1024]{1,0:T(8,128)(2,1)S(1)} all-gather(bf16[16,1024]{1,0:T(8,128)(2,1)S(1)} %copy-done), channel_id=2, replica_groups=mesh['row_0'=4,'row_1'=8,'col_0'=4,'col_1'=2] {'col_0'}, dimensions={0}, use_global_device_ids=true | all-gather | bytes 163840 | tf_op jit(solution)/shard_map/all_gather | solution.py:21
  39.6 2.0 %all-gather.1 = bf16[8,16,1024]{2,1,0:T(8,128)(2,1)S(1)} all-gather(bf16[4,16,1024]{2,1,0:T(8,128)(2,1)S(1)} %bitcast.46), channel_id=3, replica_groups=mesh['row_0'=4,'row_1'=8,'col_0'=4,'col_1'=2] {'col_1'}, dimensions={0}, use_global_device_ids=true | all-gather | bytes 393216 | tf_op jit(solution)/shard_map/all_gather | solution.py:21
  41.6 0.0 copy-start.2
  41.6 0.7 copy-done.2
  42.3 0.6 dynamic-slice.2
  43.5 0.0 copy-start.1
  43.5 0.6 copy-done.1
  44.2 0.2 dynamic-update-slice
  44.3 7.7 %all-reduce = s32[64]{0:T(128)S(1)} all-reduce(s32[64]{0:T(128)S(1)} %dynamic-update-slice), channel_id=4, replica_groups=mesh['row_0'=4,'row_1'=8,'col_0'=4,'col_1'=2] {'col_0'}, use_global_device_ids=true, to_apply=%add | all-reduce | flops 64 | bytes 512
  52.1 0.1 reshape.120
  52.1 1.8 %all-gather.4 = s32[2,4,16]{2,1,0:T(4,128)S(1)} all-gather(s32[1,4,16]{2,1,0:T(4,128)S(1)} %reshape.120), channel_id=5, replica_groups=mesh['row_0'=4,'row_1'=8,'col_0'=4,'col_1'=2] {'col_1'}, dimensions={0}, use_global_device_ids=true | all-gather | bytes 768 | tf_op jit(solution)/shard_map/all_gather | solution.py:21
  53.9 0.1 eq.35
  54.0 0.5 broadcast.94
  54.5 0.7 reduce.3
  55.2 0.1 eq.37
  55.3 0.0 all-to-all-done
  55.3 0.6 fusion.1
  55.9 0.3 exponential_reduce_fusion
  56.2 0.6 broadcast_in_dim.48
  56.8 3.7 %all-to-all-start.2 = ((f32[8,4,128]{2,1,0:T(4,128)}), f32[8,4,128]{2,1,0:T(4,128)S(1)}, u32[]{:S(2)}, u32[]{:S(2)}) async-start(f32[8,4,128]{2,1,0:T(4,128)} %broadcast_in_dim.48), calls=%async_computation.2 | async-start | bytes 32768 | tf_op jit(solution)/shard_map/all_to_all | solution.py:34
  60.6 5.4 %all-to-all-done.2 = f32[8,4,128]{2,1,0:T(4,128)S(1)} async-done(((f32[8,4,128]{2,1,0:T(4,128)}), f32[8,4,128]{2,1,0:T(4,128)S(1)}, u32[]{:S(2)}, u32[]{:S(2)}) %all-to-all-start.2) | async-done | bytes 16416 | tf_op jit(solution)/shard_map/all_to_all | solution.py:34
  66.4 0.1 dynamic-slice_bitcast_fusion
  66.5 42.0 %all-gather.5 = f32[32,16,2]{1,2,0:T(2,128)S(1)} all-gather(f32[1,16,2]{1,2,0:T(2,128)S(1)} %maximum_bitcast_fusion), channel_id=1, replica_groups=mesh['row_0'=4,'row_1'=8,'col_0'=4,'col_1'=2] {'row_0','row_1'}, dimensions={0}, use_global_device_ids=true | all-gather | bytes 4224 | tf_op jit(solution)/shard_map/all_gather | solution.py:82
  108.5 0.1 reshape.123
  108.6 0.4 fusion.2
  109.0 1.2 convolution_add_fusion
  110.2 3.5 %all-to-all-start.3 = ((f32[8,16,1024]{2,1,0:T(8,128)}), f32[8,16,1024]{2,1,0:T(8,128)S(1)}, u32[]{:S(2)}, u32[]{:S(2)}) async-start(f32[8,16,1024]{2,1,0:T(8,128)} %bitcast.23), calls=%async_computation.3 | async-start | bytes 1048576 | tf_op jit(solution)/shard_map/all_to_all | solution.py:99
  113.7 0.7 dynamic-slice_reduce_fusion
  114.4 10.7 %psum.28 = f32[]{:T(128)} all-reduce(f32[]{:T(128)} %dynamic-slice_reduce_fusion), channel_id=1, replica_groups=mesh['row_0'=4,'row_1'=8,'col_0'=4,'col_1'=2] {'row_0'}, use_global_device_ids=true, to_apply=%region_5.6 | all-reduce | flops 1 | bytes 8 | tf_op jit(solution)/shard_map/psum | solution.py:74
  125.1 15.6 %psum.29 = f32[]{:T(128)} all-reduce(f32[]{:T(128)} %psum.28), channel_id=1, replica_groups=mesh['row_0'=4,'row_1'=8,'col_0'=4,'col_1'=2] {'row_1'}, use_global_device_ids=true, to_apply=%region_6.7 | all-reduce | flops 1 | bytes 8 | tf_op jit(solution)/shard_map/psum | solution.py:74
  140.7 11.5 %psum.30 = f32[]{:T(128)} all-reduce(f32[]{:T(128)} %psum.29), channel_id=1, replica_groups=mesh['row_0'=4,'row_1'=8,'col_0'=4,'col_1'=2] {'col_0'}, use_global_device_ids=true, to_apply=%region_7.8 | all-reduce | flops 1 | bytes 8 | tf_op jit(solution)/shard_map/psum | solution.py:74
  152.2 3.1 %psum.31 = f32[]{:T(128)} all-reduce(f32[]{:T(128)} %psum.30), channel_id=1, replica_groups=mesh['row_0'=4,'row_1'=8,'col_0'=4,'col_1'=2] {'col_1'}, use_global_device_ids=true, to_apply=%region_8.9 | all-reduce | flops 1 | bytes 8 | tf_op jit(solution)/shard_map/psum | solution.py:74
  156.0 0.0 all-to-all-done.3
  156.0 0.6 multiply_convert_fusion.4
  (34 shorter events, 0.5 us)
Async XLA Ops:
  0.6 20.5 %copy-start = (bf16[16,1024]{1,0:T(8,128)(2,1)S(1)}, bf16[16,1024]{1,0:T(8,128)(2,1)}, u32[]{:S(2)}) copy-start(bf16[16,1024]{1,0:T(8,128)(2,1)} %param.2) | copy-start | bytes 98308
  22.2 33.1 %all-to-all-start = ((bf16[32,16,1024]{2,1,0:T(8,128)(2,1)}), bf16[32,16,1024]{2,1,0:T(8,128)(2,1)S(1)}, u32[]{:S(2)}, u32[]{:S(2)}) async-start(bf16[32,16,1024]{2,1,0:T(8,128)(2,1)} %broadcast_in_dim.45), calls=%async_computation | async-start | bytes 2097152 | tf_op jit(solution)/shard_map/all_to_all | solution.py:34
  41.6 0.7 copy-start.2
  43.5 0.7 copy-start.1
  56.8 9.1 %all-to-all-start.2 = ((f32[8,4,128]{2,1,0:T(4,128)}), f32[8,4,128]{2,1,0:T(4,128)S(1)}, u32[]{:S(2)}, u32[]{:S(2)}) async-start(f32[8,4,128]{2,1,0:T(4,128)} %broadcast_in_dim.48), calls=%async_computation.2 | async-start | bytes 32768 | tf_op jit(solution)/shard_map/all_to_all | solution.py:34
  110.2 45.7 %all-to-all-start.3 = ((f32[8,16,1024]{2,1,0:T(8,128)}), f32[8,16,1024]{2,1,0:T(8,128)S(1)}, u32[]{:S(2)}, u32[]{:S(2)}) async-start(f32[8,16,1024]{2,1,0:T(8,128)} %bitcast.23), calls=%async_computation.3 | async-start | bytes 1048576 | tf_op jit(solution)/shard_map/all_to_all | solution.py:99
where the time goes:
time: 161 us; the launch traced here: 158 us
  blocking collectives  126 us (78%)
  starting transfers between devices  12.2 us (8%)
  local copies, waits for them, and re-layouts  5.82 us (4%)
  waiting for transfers between devices  5.36 us (3%)
  between operations  3.23 us (2%)
  other arithmetic  2.42 us (2%)
  matrix products  2.21 us (1%)
    all_gather x1, blocking collectives, rows_first(): result = lax.all_gather(both, axis, axis=0, tiled=True)  42 us
    psum x4, blocking collectives, one_axis_at_a_time(): x = lax.psum(x, axis)  40.9 us
    all_to_all x1, blocking collectives, sent_to_all(): return lax.all_to_all(copies, axis, split_axis=0, concat_axis=0, tiled=True)  19.8 us
    all_gather x3, blocking collectives, stacked_from(): parts = lax.all_gather(parts, axes[k])  16.1 us
    all_to_all x2, starting transfers between devices, sent_to_all(): return lax.all_to_all(copies, axis, split_axis=0, concat_axis=0, tiled=True)  8.73 us
    unnamed x1, blocking collectives  7.71 us
    all_to_all x2, waiting for transfers between devices, sent_to_all(): return lax.all_to_all(copies, axis, split_axis=0, concat_axis=0, tiled=True)  5.36 us
    all_to_all x1, starting transfers between devices, sent_and_summed(): lax.all_to_all(parts, axis, split_axis=0, concat_axis=0, tiled=True)  3.49 us
  transfers between devices with their start and end apart: 3, of which 1 were waited for; matrix products, arithmetic and copies ran while one was open for 2% of the time, Pallas kernels for 0%

commit v1 on v0

v1 whole, which is shorter than its diff:
```python
import functools

import jax
import jax.numpy as jnp
from jax import lax
from jax.experimental import pallas as pl
from jax.experimental.pallas import tpu as pltpu
from jax.sharding import Mesh
from jax.sharding import PartitionSpec as P

MESH = pl.DeviceIdType.MESH
ALL = ("y", "z", "x", "c")
IDS = 128
HALF = 32
LANES = 128


def wait_bytes(ref, sem):
    pltpu.make_async_copy(ref, ref, sem).wait()


def kernel(
    sizes,
    emb_ref,
    ids_ref,
    loss_ref,
    grad_ref,
    keys,
    queries,
    ids_smem,
    col_mine,
    col_all,
    row_mine,
    row_all,
    part_mine,
    part_all,
    loss_mine,
    loss_all,
    in_sem,
    key_send,
    key_recv,
    fwd_send,
    fwd_recv,
    query_send,
    query_recv,
    col_sem,
    row_sem,
    part_sem,
    loss_sem,
):
    ny, nz, nx, nc, rows, width = sizes
    chips = ny * nx
    plane = chips * nc
    n_query, n_key = nz * rows, plane * rows
    whole = n_query * plane
    y, z, x, c = (lax.axis_index(a) for a in ALL)
    chip = y * nx + x
    mine = chip * nc + c
    sibling = (y, z, x, 1 - c)

    def in_plane(k):
        return (k // (nx * nc), z, (k // nc) % nx, k % nc)

    def key_slot(k):
        return keys.at[pl.ds(pl.multiple_of(k * rows, rows), rows)]

    def query_slot(k):
        return queries.at[pl.ds(pl.multiple_of(k * rows, rows), rows)]

    load = pltpu.make_async_copy(emb_ref, key_slot(mine).at[:, pl.ds(0, width)], in_sem.at[0])
    load.start()
    load_ids = pltpu.make_async_copy(ids_ref, ids_smem, in_sem.at[1])
    load_ids.start()

    with jax.named_scope("barrier"):
        barrier = pltpu.get_barrier_semaphore()

        def greet_plane(k, _):
            pl.semaphore_signal(
                barrier, inc=1, device_id=in_plane(lax.rem(mine + k, plane)), device_id_type=MESH
            )
            return 0

        def greet_ring(k, _):
            pl.semaphore_signal(
                barrier, inc=1, device_id=(y, lax.rem(z + k, nz), x, c), device_id_type=MESH
            )
            return 0

        lax.fori_loop(1, plane, greet_plane, 0)
        lax.fori_loop(1, nz, greet_ring, 0)

        load_ids.wait()
        at_row = lax.broadcasted_iota(jnp.int32, (rows, IDS), 0)
        lane = lax.broadcasted_iota(jnp.int32, (rows, IDS), 1)
        ids = jnp.zeros((rows, IDS), jnp.int32)
        for r in range(rows):
            ids = jnp.where(at_row == r, ids_smem[r], ids)
        hot = jnp.logical_or(
            lane == lax.shift_right_logical(ids, 5), lane == HALF + jnp.bitwise_and(ids, HALF - 1)
        )
        key_slot(mine)[:, width:] = jnp.where(hot, 1.0, 0.0).astype(jnp.bfloat16)
        load.wait()
        query_slot(z)[...] = key_slot(mine)[...]
        pl.semaphore_wait(barrier, plane - 1 + nz - 1)

    def query_copy(k):
        return pltpu.make_async_remote_copy(
            src_ref=key_slot(mine),
            dst_ref=query_slot(z),
            send_sem=query_send.at[k],
            recv_sem=query_recv.at[k],
            device_id=(y, lax.rem(z + k, nz), x, c),
            device_id_type=MESH,
        )

    def key_copy(k):
        to = lax.rem(chip + k, chips)
        return pltpu.make_async_remote_copy(
            src_ref=key_slot(mine),
            dst_ref=key_slot(mine),
            send_sem=key_send.at[k],
            recv_sem=key_recv.at[k],
            device_id=(to // nx, z, to % nx, c),
            device_id_type=MESH,
        )

    def passed_on(k):
        slot = key_slot(lax.rem(chip + chips - k, chips) * nc + c)
        return pltpu.make_async_remote_copy(
            src_ref=slot,
            dst_ref=slot,
            send_sem=fwd_send.at[k],
            recv_sem=fwd_recv.at[k],
            device_id=sibling,
            device_id_type=MESH,
        )

    def started(copy):
        def body(k, _):
            copy(k).start()
            return 0

        return body

    with jax.named_scope("gather_start"):
        passed_on(0).start()
        lax.fori_loop(1, nz, started(query_copy), 0)
        lax.fori_loop(1, chips, started(key_copy), 0)

    with jax.named_scope("gather_pass_on"):

        def pass_on(k, _):
            key_copy(k).wait_recv()
            passed_on(k).start()
            return 0

        lax.fori_loop(1, chips, pass_on, 0)

    with jax.named_scope("gather_wait"):

        def arrived(copy):
            def body(k, _):
                copy(k).wait_recv()
                return 0

            return body

        lax.fori_loop(1, nz, arrived(query_copy), 0)
        lax.fori_loop(0, chips, arrived(passed_on), 0)

    contract_last = (((1,), (1,)), ((), ()))
    with jax.named_scope("scores"):
        scores = lax.dot_general(
            queries[:, :width], keys[:, :width], contract_last, preferred_element_type=jnp.float32
        ) * (1.0 / width**0.5)
        same = (
            lax.dot_general(
                queries[:, width:],
                keys[:, width:],
                contract_last,
                preferred_element_type=jnp.float32,
            )
            > 1.5
        )
        q_at = lax.broadcasted_iota(jnp.int32, (n_query, n_key), 0)
        k_at = lax.broadcasted_iota(jnp.int32, (n_query, n_key), 1)
        selfs = jnp.logical_and(k_at - q_at == rows * (mine - z), q_at // rows == z)
        positive = jnp.logical_and(same, jnp.logical_not(selfs))
        pos = jnp.where(positive, 1.0, 0.0)
        masked = jnp.where(selfs, jnp.float32(-1e30), scores)

    with jax.named_scope("stats"):
        peak = jnp.max(masked, axis=0, keepdims=True)
        col_lse = peak + jnp.log(jnp.sum(jnp.exp(masked - peak), axis=0, keepdims=True))
        col_count = jnp.sum(pos, axis=0, keepdims=True)
        for r in range(n_key // LANES):
            at = slice(r * LANES, (r + 1) * LANES)
            col_mine[0, r : r + 1, :] = col_lse[:, at]
            col_mine[1, r : r + 1, :] = col_count[:, at]
        col_all[pl.ds(mine, 1)] = col_mine[...][None]

    def col_copy(k):
        return pltpu.make_async_remote_copy(
            src_ref=col_mine,
            dst_ref=col_all.at[mine],
            send_sem=col_sem.at[0],
            recv_sem=col_sem.at[1],
            device_id=in_plane(lax.rem(mine + k, plane)),
            device_id_type=MESH,
        )

    def row_copy(k):
        return pltpu.make_async_remote_copy(
            src_ref=row_mine,
            dst_ref=row_all.at[z],
            send_sem=row_sem.at[0],
            recv_sem=row_sem.at[1],
            device_id=(y, lax.rem(z + k, nz), x, c),
            device_id_type=MESH,
        )

    with jax.named_scope("col_start"):
        lax.fori_loop(1, plane, started(col_copy), 0)

    with jax.named_scope("row_stats"):
        peak = jnp.max(masked, axis=1, keepdims=True)
        row_lse = peak + jnp.log(jnp.sum(jnp.exp(masked - peak), axis=1, keepdims=True))
        row_possum = jnp.sum(pos * scores, axis=1, keepdims=True)
        row_count = jnp.sum(pos, axis=1, keepdims=True)
        lane = lax.broadcasted_iota(jnp.int32, (n_query, LANES), 1)
        tall = jnp.where(lane == 0, row_lse, jnp.where(lane == 1, row_possum, row_count))
        row_mine[...] = jnp.transpose(tall)[:4]
        row_all[pl.ds(z, 1)] = row_mine[...][None]
        lax.fori_loop(1, nz, started(row_copy), 0)

    with jax.named_scope("stats_wait"):
        wait_bytes(col_all.at[pl.ds(0, plane - 1)], col_sem.at[1])
        wait_bytes(row_all.at[pl.ds(0, nz - 1)], row_sem.at[1])

    def log_sum_exp(parts):
        peak = jnp.max(parts, axis=0)
        return peak + jnp.log(jnp.sum(jnp.exp(parts - peak[None]), axis=0))

    with jax.named_scope("weights"):
        key_lse = log_sum_exp(col_all[:, 0])
        key_inverse = 1.0 / jnp.sum(col_all[:, 1], axis=0)
        query_lse = log_sum_exp(row_all[:, 0:1])
        query_possum = jnp.sum(row_all[:, 1:2], axis=0)
        query_inverse = 1.0 / jnp.sum(row_all[:, 2:3], axis=0)
        tall_lse = jnp.transpose(jnp.broadcast_to(query_lse, (LANES, n_query)))[:, :1]
        tall_inverse = jnp.transpose(jnp.broadcast_to(query_inverse, (LANES, n_query)))[:, :1]
        flat_lse = jnp.concatenate([key_lse[r : r + 1] for r in range(n_key // LANES)], axis=1)
        flat_inverse = jnp.concatenate(
            [key_inverse[r : r + 1] for r in range(n_key // LANES)], axis=1
        )
        weight = (jnp.exp(masked - tall_lse) - pos * tall_inverse) * (1.0 / whole)
        mirrored = (jnp.exp(masked - flat_lse) - pos * flat_inverse) * (1.0 / whole)

    with jax.named_scope("gradient"):
        both = jnp.concatenate([weight.astype(jnp.bfloat16), mirrored.astype(jnp.bfloat16)], axis=0)
        terms = jnp.dot(both, keys[:, :width], preferred_element_type=jnp.float32)
        terms = (terms[:n_query] + terms[n_query:]) * (1.0 / width**0.5)
        part_mine[...] = terms.astype(jnp.bfloat16)

    def part_copy(k):
        to = lax.rem(z + k, nz)
        return pltpu.make_async_remote_copy(
            src_ref=part_mine.at[pl.ds(pl.multiple_of(to * rows, rows), rows)],
            dst_ref=part_all.at[z],
            send_sem=part_sem.at[0],
            recv_sem=part_sem.at[1],
            device_id=(y, to, x, c),
            device_id_type=MESH,
        )

    def loss_copy(k):
        return pltpu.make_async_remote_copy(
            src_ref=loss_mine,
            dst_ref=loss_all.at[mine],
            send_sem=loss_sem.at[0],
            recv_sem=loss_sem.at[1],
            device_id=in_plane(lax.rem(mine + k, plane)),
            device_id_type=MESH,
        )

    with jax.named_scope("reduce_start"):
        lax.fori_loop(1, nz, started(part_copy), 0)
        part_all[pl.ds(z, 1)] = part_mine[pl.ds(pl.multiple_of(z * rows, rows), rows), :][None]
        loss_mine[...] = query_lse - query_possum * query_inverse
        loss_all[pl.ds(mine, 1)] = loss_mine[...][None]
        lax.fori_loop(1, plane, started(loss_copy), 0)

    with jax.named_scope("sends_wait"):

        def sent(copy):
            def body(k, _):
                copy(k).wait_send()
                return 0

            return body

        lax.fori_loop(1, nz, sent(query_copy), 0)
        lax.fori_loop(1, chips, sent(key_copy), 0)
        lax.fori_loop(0, chips, sent(passed_on), 0)
        wait_bytes(col_all.at[pl.ds(0, plane - 1)], col_sem.at[0])
        wait_bytes(row_all.at[pl.ds(0, nz - 1)], row_sem.at[0])
        wait_bytes(part_all.at[pl.ds(0, nz - 1)], part_sem.at[0])
        wait_bytes(loss_all.at[pl.ds(0, plane - 1)], loss_sem.at[0])

    with jax.named_scope("loss_wait"):
        wait_bytes(loss_all.at[pl.ds(0, plane - 1)], loss_sem.at[1])
        total = jnp.sum(loss_all[...], axis=0)
        loss_ref[...] = jnp.sum(total, axis=1, keepdims=True) * (1.0 / whole)

    with jax.named_scope("reduce_wait"):
        wait_bytes(part_all.at[pl.ds(0, nz - 1)], part_sem.at[1])
        grad_ref[...] = jnp.sum(part_all[...].astype(jnp.float32), axis=0).astype(jnp.bfloat16)


def on_device(embeddings, group_ids):
    ny, nz, nx, nc = (lax.axis_size(a) for a in ALL)
    rows, width = embeddings.shape
    chips = ny * nx
    plane = chips * nc
    n_query, n_key = nz * rows, plane * rows
    dma = pltpu.SemaphoreType.DMA
    loss, grad = pl.pallas_call(
        functools.partial(kernel, (ny, nz, nx, nc, rows, width)),
        out_shape=(
            jax.ShapeDtypeStruct((1, 1), jnp.float32),
            jax.ShapeDtypeStruct((rows, width), jnp.bfloat16),
        ),
        in_specs=[pl.BlockSpec(memory_space=pl.ANY)] * 2,
        out_specs=(
            pl.BlockSpec(memory_space=pltpu.VMEM),
            pl.BlockSpec(memory_space=pltpu.VMEM),
        ),
        scratch_shapes=[
            pltpu.VMEM((n_key, width + IDS), jnp.bfloat16),
            pltpu.VMEM((n_query, width + IDS), jnp.bfloat16),
            pltpu.SMEM((rows,), jnp.int32),
            pltpu.VMEM((2, n_key // LANES, LANES), jnp.float32),
            pltpu.VMEM((plane, 2, n_key // LANES, LANES), jnp.float32),
            pltpu.VMEM((4, n_query), jnp.float32),
            pltpu.VMEM((nz, 4, n_query), jnp.float32),
            pltpu.VMEM((n_query, width), jnp.bfloat16),
            pltpu.VMEM((nz, rows, width), jnp.bfloat16),
            pltpu.VMEM((1, n_query), jnp.float32),
            pltpu.VMEM((plane, 1, n_query), jnp.float32),
            dma((2,)),
            dma((chips,)),
            dma((chips,)),
            dma((chips,)),
            dma((chips,)),
            dma((nz,)),
            dma((nz,)),
            dma((2,)),
            dma((2,)),
            dma((2,)),
            dma((2,)),
        ],
        compiler_params=pltpu.CompilerParams(
            collective_id=0, has_side_effects=True, vmem_limit_bytes=32 * 1024 * 1024
        ),
    )(embeddings, group_ids)
    return loss.reshape(()), grad


def solution(mesh):
    split = Mesh(mesh.devices.reshape(4, 8, 4, 2), ALL)
    return jax.shard_map(
        on_device,
        mesh=split,
        in_specs=(P(ALL, None), P(ALL)),
        out_specs=(P(), P(ALL, None)),
        check_vma=False,
    )
```

time: 161 us -> 41.7 us (0.26)
  the two profiles are of different devices: /device:TPU:32 before, /device:TPU:1 now
where the time goes in v1:
time: 41.7 us; the launch traced here: 41.6 us
  Pallas kernels  37.1 us (89%)
  between operations  2.41 us (6%)
  local copies, waits for them, and re-layouts  2.02 us (5%)
    pallas_call x1, Pallas kernels, on_device(): pl.pallas_call(functools.partial(kernel, (ny, nz, nx, nc, rows, width)),...  37.1 us
    unnamed x5, local copies, waits for them, and re-layouts  2.02 us

profile of v1, /device:TPU:1, one launch (start us, length us, event | category | flops | bytes accessed | tf_op | source)
XLA Modules:
  0.0 41.6 jit_solution(8225185779521736955)
XLA Ops:
  0.6 0.0 copy-start
  0.6 0.7 %copy-done = bf16[16,1024]{1,0:T(8,128)(2,1)S(1)} copy-done((bf16[16,1024]{1,0:T(8,128)(2,1)S(1)}, bf16[16,1024]{1,0:T(8,128)(2,1)}, u32[]{:S(2)}) %copy-start) | copy-done | bytes 32792
  1.4 0.0 copy-start.1
  1.4 0.7 %copy-done.1 = s32[16]{0:T(128)S(1)} copy-done((s32[16]{0:T(128)S(1)}, s32[16]{0:T(128)}, u32[]{:S(2)}) %copy-start.1) | copy-done | bytes 88
  2.0 37.1 %shard_map.41 = (f32[1,1]{1,0:T(1,128)}, bf16[16,1024]{1,0:T(8,128)(2,1)S(1)}) custom-call(bf16[16,1024]{1,0:T(8,128)(2,1)S(1)} %copy-done, s32[16]{0:T(128)S(1)} %copy-done.1), custom_call_target="tpu_custom_call" | custom-call | tf_op jit(solution)/shard_map/pallas_call | solution.py:328
  39.8 0.6 %copy.7 = bf16[16,1024]{1,0:T(8,128)(2,1)} copy(bf16[16,1024]{1,0:T(8,128)(2,1)S(1)} %get-tuple-element.9) | data formatting | bytes 65536
Async XLA Ops:
  0.6 0.8 %copy-start = (bf16[16,1024]{1,0:T(8,128)(2,1)S(1)}, bf16[16,1024]{1,0:T(8,128)(2,1)}, u32[]{:S(2)}) copy-start(bf16[16,1024]{1,0:T(8,128)(2,1)} %emb_ref.1) | copy-start | bytes 98308
  1.4 0.7 %copy-start.1 = (s32[16]{0:T(128)S(1)}, s32[16]{0:T(128)}, u32[]{:S(2)}) copy-start(s32[16]{0:T(128)} %ids_ref.1) | copy-start | bytes 196

commit v2 on v1

--- a/solution.py
+++ b/solution.py
@@ -58,8 +58,17 @@
     mine = chip * nc + c
     sibling = (y, z, x, 1 - c)
 
-    def in_plane(k):
-        return (k // (nx * nc), z, (k // nc) % nx, k % nc)
+    ring = sorted(range(1, nz), key=lambda k: -min(k, nz - k))
+    others = [(dy, dx, dc) for dy in range(ny) for dx in range(nx) for dc in range(nc)][1:]
+    others.sort(key=lambda o: -min(o[0], ny - o[0]) - min(o[1], nx - o[1]))
+    chips_away = [(dy, dx) for dy, dx, dc in others if dc == 0]
+
+    def in_ring(k):
+        return (y, (z + k) % nz, x, c)
+
+    def in_plane(offset):
+        dy, dx, dc = offset
+        return ((y + dy) % ny, z, (x + dx) % nx, c if dc == 0 else 1 - c)
 
     def key_slot(k):
         return keys.at[pl.ds(pl.multiple_of(k * rows, rows), rows)]
@@ -75,20 +84,12 @@
     with jax.named_scope("barrier"):
         barrier = pltpu.get_barrier_semaphore()
 
-        def greet_plane(k, _):
-            pl.semaphore_signal(
-                barrier, inc=1, device_id=in_plane(lax.rem(mine + k, plane)), device_id_type=MESH
-            )
-            return 0
-
-        def greet_ring(k, _):
-            pl.semaphore_signal(
-                barrier, inc=1, device_id=(y, lax.rem(z + k, nz), x, c), device_id_type=MESH
-            )
-            return 0
-
-        lax.fori_loop(1, plane, greet_plane, 0)
-        lax.fori_loop(1, nz, greet_ring, 0)
+        for k in ring[:1]:
+            pl.semaphore_signal(barrier, inc=1, device_id=in_ring(k), device_id_type=MESH)
+        for offset in others:
+            pl.semaphore_signal(barrier, inc=1, device_id=in_plane(offset), device_id_type=MESH)
+        for k in ring[1:]:
+            pl.semaphore_signal(barrier, inc=1, device_id=in_ring(k), device_id_type=MESH)
 
         load_ids.wait()
         at_row = lax.broadcasted_iota(jnp.int32, (rows, IDS), 0)
@@ -110,64 +111,52 @@
             dst_ref=query_slot(z),
             send_sem=query_send.at[k],
             recv_sem=query_recv.at[k],
-            device_id=(y, lax.rem(z + k, nz), x, c),
-            device_id_type=MESH,
-        )
-
-    def key_copy(k):
-        to = lax.rem(chip + k, chips)
+            device_id=in_ring(k),
+            device_id_type=MESH,
+        )
+
+    def key_copy(offset):
         return pltpu.make_async_remote_copy(
             src_ref=key_slot(mine),
             dst_ref=key_slot(mine),
-            send_sem=key_send.at[k],
-            recv_sem=key_recv.at[k],
-            device_id=(to // nx, z, to % nx, c),
-            device_id_type=MESH,
-        )
-
-    def passed_on(k):
-        slot = key_slot(lax.rem(chip + chips - k, chips) * nc + c)
+            send_sem=key_send.at[offset[0] * nx + offset[1]],
+            recv_sem=key_recv.at[offset[0] * nx + offset[1]],
+            device_id=in_plane((*offset, 0)),
+            device_id_type=MESH,
+        )
+
+    def passed_on(offset):
+        came_from = (y + ny - offset[0]) % ny * nx + (x + nx - offset[1]) % nx
+        slot = key_slot(came_from * nc + c)
         return pltpu.make_async_remote_copy(
             src_ref=slot,
             dst_ref=slot,
-            send_sem=fwd_send.at[k],
-            recv_sem=fwd_recv.at[k],
+            send_sem=fwd_send.at[offset[0] * nx + offset[1]],
+            recv_sem=fwd_recv.at[offset[0] * nx + offset[1]],
             device_id=sibling,
             device_id_type=MESH,
         )
 
-    def started(copy):
-        def body(k, _):
-            copy(k).start()
-            return 0
-
-        return body
-
     with jax.named_scope("gather_start"):
-        passed_on(0).start()
-        lax.fori_loop(1, nz, started(query_copy), 0)
-        lax.fori_loop(1, chips, started(key_copy), 0)
-
-    with jax.named_scope("gather_pass_on"):
-
-        def pass_on(k, _):
-            key_copy(k).wait_recv()
-            passed_on(k).start()
-            return 0
-
-        lax.fori_loop(1, chips, pass_on, 0)
+        query_copy(ring[0]).start()
+        for offset in chips_away[:5]:
+            key_copy(offset).start()
+        for k in ring[1:]:
+            query_copy(k).start()
+        for offset in chips_away[5:]:
+            key_copy(offset).start()
+        passed_on((0, 0)).start()
+
+    with jax.named_scope("key_pass_on"):
+        for offset in chips_away[::-1]:
+            key_copy(offset).wait_recv()
+            passed_on(offset).start()
 
     with jax.named_scope("gather_wait"):
-
-        def arrived(copy):
-            def body(k, _):
-                copy(k).wait_recv()
-                return 0
-
-            return body
-
-        lax.fori_loop(1, nz, arrived(query_copy), 0)
-        lax.fori_loop(0, chips, arrived(passed_on), 0)
+        for k in ring[::-1]:
+            query_copy(k).wait_recv()
+        for offset in [(0, 0)] + chips_away[::-1]:
+            passed_on(offset).wait_recv()
 
     contract_last = (((1,), (1,)), ((), ()))
     with jax.named_scope("scores"):
@@ -200,13 +189,13 @@
             col_mine[1, r : r + 1, :] = col_count[:, at]
         col_all[pl.ds(mine, 1)] = col_mine[...][None]
 
-    def col_copy(k):
+    def col_copy(offset):
         return pltpu.make_async_remote_copy(
             src_ref=col_mine,
             dst_ref=col_all.at[mine],
             send_sem=col_sem.at[0],
             recv_sem=col_sem.at[1],
-            device_id=in_plane(lax.rem(mine + k, plane)),
+            device_id=in_plane(offset),
             device_id_type=MESH,
         )
 
@@ -216,12 +205,13 @@
             dst_ref=row_all.at[z],
             send_sem=row_sem.at[0],
             recv_sem=row_sem.at[1],
-            device_id=(y, lax.rem(z + k, nz), x, c),
+            device_id=in_ring(k),
             device_id_type=MESH,
         )
 
     with jax.named_scope("col_start"):
-        lax.fori_loop(1, plane, started(col_copy), 0)
+        for offset in others:
+            col_copy(offset).start()
 
     with jax.named_scope("row_stats"):
         peak = jnp.max(masked, axis=1, keepdims=True)
@@ -232,7 +222,8 @@
         tall = jnp.where(lane == 0, row_lse, jnp.where(lane == 1, row_possum, row_count))
         row_mine[...] = jnp.transpose(tall)[:4]
         row_all[pl.ds(z, 1)] = row_mine[...][None]
-        lax.fori_loop(1, nz, started(row_copy), 0)
+        for k in ring:
+            row_copy(k).start()
 
     with jax.named_scope("stats_wait"):
         wait_bytes(col_all.at[pl.ds(0, plane - 1)], col_sem.at[1])
@@ -263,10 +254,9 @@
         terms = (terms[:n_query] + terms[n_query:]) * (1.0 / width**0.5)
         part_mine[...] = terms.astype(jnp.bfloat16)
 
-    def part_copy(k):
-        to = lax.rem(z + k, nz)
-        return pltpu.make_async_remote_copy(
-            src_ref=part_mine.at[pl.ds(pl.multiple_of(to * rows, rows), rows)],
+    def part_copy(to):
+        return pltpu.make_async_remote_copy(
+            src_ref=part_mine.at[pl.ds(to * rows, rows)],
             dst_ref=part_all.at[z],
             send_sem=part_sem.at[0],
             recv_sem=part_sem.at[1],
@@ -274,44 +264,53 @@
             device_id_type=MESH,
         )
 
-    def loss_copy(k):
+    def loss_copy(offset):
         return pltpu.make_async_remote_copy(
             src_ref=loss_mine,
             dst_ref=loss_all.at[mine],
             send_sem=loss_sem.at[0],
             recv_sem=loss_sem.at[1],
-            device_id=in_plane(lax.rem(mine + k, plane)),
+            device_id=in_plane(offset),
             device_id_type=MESH,
         )
 
     with jax.named_scope("reduce_start"):
-        lax.fori_loop(1, nz, started(part_copy), 0)
+        for to in range(nz):
+
+            @pl.when(z != to)
+            def _():
+                part_copy(to).start()
+
         part_all[pl.ds(z, 1)] = part_mine[pl.ds(pl.multiple_of(z * rows, rows), rows), :][None]
+
+    with jax.named_scope("loss_start"):
         loss_mine[...] = query_lse - query_possum * query_inverse
         loss_all[pl.ds(mine, 1)] = loss_mine[...][None]
-        lax.fori_loop(1, plane, started(loss_copy), 0)
-
-    with jax.named_scope("sends_wait"):
-
-        def sent(copy):
-            def body(k, _):
-                copy(k).wait_send()
-                return 0
-
-            return body
-
-        lax.fori_loop(1, nz, sent(query_copy), 0)
-        lax.fori_loop(1, chips, sent(key_copy), 0)
-        lax.fori_loop(0, chips, sent(passed_on), 0)
+        for offset in others:
+            loss_copy(offset).start()
+
+    with jax.named_scope("gather_sent"):
+        for k in ring:
+            query_copy(k).wait_send()
+        for offset in chips_away:
+            key_copy(offset).wait_send()
+        for offset in [(0, 0)] + chips_away:
+            passed_on(offset).wait_send()
+
+    with jax.named_scope("stats_sent"):
         wait_bytes(col_all.at[pl.ds(0, plane - 1)], col_sem.at[0])
         wait_bytes(row_all.at[pl.ds(0, nz - 1)], row_sem.at[0])
+
+    with jax.named_scope("part_sent"):
         wait_bytes(part_all.at[pl.ds(0, nz - 1)], part_sem.at[0])
+
+    with jax.named_scope("loss_sent"):
         wait_bytes(loss_all.at[pl.ds(0, plane - 1)], loss_sem.at[0])
 
     with jax.named_scope("loss_wait"):
         wait_bytes(loss_all.at[pl.ds(0, plane - 1)], loss_sem.at[1])
         total = jnp.sum(loss_all[...], axis=0)
-        loss_ref[...] = jnp.sum(total, axis=1, keepdims=True) * (1.0 / whole)
+        loss_ref[...] = jnp.broadcast_to(jnp.sum(total, axis=1, keepdims=True) * (1.0 / whole), (8, 128))
 
     with jax.named_scope("reduce_wait"):
         wait_bytes(part_all.at[pl.ds(0, nz - 1)], part_sem.at[1])
@@ -328,10 +327,10 @@
     loss, grad = pl.pallas_call(
         functools.partial(kernel, (ny, nz, nx, nc, rows, width)),
         out_shape=(
-            jax.ShapeDtypeStruct((1, 1), jnp.float32),
-            jax.ShapeDtypeStruct((rows, width), jnp.bfloat16),
+            pltpu.VMEM((8, 128), jnp.float32),
+            pltpu.VMEM((rows, width), jnp.bfloat16),
         ),
-        in_specs=[pl.BlockSpec(memory_space=pl.ANY)] * 2,
+        in_specs=[pl.BlockSpec(memory_space=pltpu.HBM)] * 2,
         out_specs=(
             pl.BlockSpec(memory_space=pltpu.VMEM),
             pl.BlockSpec(memory_space=pltpu.VMEM),
@@ -361,9 +360,23 @@
             dma((2,)),
         ],
         compiler_params=pltpu.CompilerParams(
-            collective_id=0, has_side_effects=True, vmem_limit_bytes=32 * 1024 * 1024
+            collective_id=0, has_side_effects=True, vmem_limit_bytes=60 * 1024 * 1024
         ),
     )(embeddings, group_ids)
+
+    def finish(loss_in, grad_in, loss_out, grad_out):
+        loss_out[...] = loss_in[:1, :1]
+        grad_out[...] = grad_in[...]
+
+    loss, grad = pl.pallas_call(
+        finish,
+        out_shape=(
+            jax.ShapeDtypeStruct((1, 1), jnp.float32),
+            jax.ShapeDtypeStruct((rows, width), jnp.bfloat16),
+        ),
+        in_specs=[pl.BlockSpec(memory_space=pltpu.VMEM)] * 2,
+        compiler_params=pltpu.CompilerParams(vmem_limit_bytes=1024 * 1024),
+    )(loss, grad)
     return loss.reshape(()), grad
 
 

time: 41.7 us -> 36 us (0.86)
  the two profiles are of different devices: /device:TPU:1 before, /device:TPU:32 now
where the time goes in v2:
time: 36 us; the launch traced here: 35.9 us
  Pallas kernels  35.2 us (98%)
  between operations  0.64 us (2%)
    pallas_call x1, Pallas kernels, on_device(): pl.pallas_call(functools.partial(kernel, (ny, nz, nx, nc, rows, width)),...  34.6 us

profile of v2, /device:TPU:32, one launch (start us, length us, event | category | flops | bytes accessed | tf_op | source)
XLA Modules:
  0.0 35.9 jit_solution(13187156657187209359)
XLA Ops:
  0.6 34.6 %shard_map.41 = (f32[8,128]{1,0:T(8,128)S(1)}, bf16[16,1024]{1,0:T(8,128)(2,1)S(1)}) custom-call(bf16[16,1024]{1,0:T(8,128)(2,1)} %emb_ref.1, s32[16]{0:T(128)} %ids_ref.1), custom_call_target="tpu_custom_call" | custom-call | tf_op jit(solution)/shard_map/pallas_call | solution.py:327
  35.3 0.6 %shard_map.42 = (f32[1,1]{1,0:T(1,128)}, bf16[16,1024]{1,0:T(8,128)(2,1)}) custom-call(f32[8,128]{1,0:T(8,128)S(1)} %get-tuple-element.6.loss_in, bf16[16,1024]{1,0:T(8,128)(2,1)S(1)} %get-tuple-element.7.grad_in), custom_call_target="tpu_custom_call" | custom-call | tf_op jit(solution)/shard_map/pallas_call | solution.py:371

commit v3 on v2

--- a/solution.py
+++ b/solution.py
@@ -10,8 +10,6 @@
 
 MESH = pl.DeviceIdType.MESH
 ALL = ("y", "z", "x", "c")
-IDS = 128
-HALF = 32
 LANES = 128
 
 
@@ -28,6 +26,9 @@
     keys,
     queries,
     ids_smem,
+    ids_mine,
+    ids_plane,
+    ids_ring,
     col_mine,
     col_all,
     row_mine,
@@ -43,6 +44,8 @@
     fwd_recv,
     query_send,
     query_recv,
+    ids_plane_sem,
+    ids_ring_sem,
     col_sem,
     row_sem,
     part_sem,
@@ -51,11 +54,10 @@
     ny, nz, nx, nc, rows, width = sizes
     chips = ny * nx
     plane = chips * nc
-    n_query, n_key = nz * rows, plane * rows
+    n_query, n_key, n_half = nz * rows, plane * rows, chips * rows
     whole = n_query * plane
     y, z, x, c = (lax.axis_index(a) for a in ALL)
     chip = y * nx + x
-    mine = chip * nc + c
     sibling = (y, z, x, 1 - c)
 
     ring = sorted(range(1, nz), key=lambda k: -min(k, nz - k))
@@ -70,13 +72,14 @@
         dy, dx, dc = offset
         return ((y + dy) % ny, z, (x + dx) % nx, c if dc == 0 else 1 - c)
 
-    def key_slot(k):
-        return keys.at[pl.ds(pl.multiple_of(k * rows, rows), rows)]
+    def key_slot(half, k):
+        start = half * n_half + pl.multiple_of(k * rows, rows)
+        return keys.at[pl.ds(start, rows)]
 
     def query_slot(k):
         return queries.at[pl.ds(pl.multiple_of(k * rows, rows), rows)]
 
-    load = pltpu.make_async_copy(emb_ref, key_slot(mine).at[:, pl.ds(0, width)], in_sem.at[0])
+    load = pltpu.make_async_copy(emb_ref, key_slot(0, chip), in_sem.at[0])
     load.start()
     load_ids = pltpu.make_async_copy(ids_ref, ids_smem, in_sem.at[1])
     load_ids.start()
@@ -92,107 +95,191 @@
             pl.semaphore_signal(barrier, inc=1, device_id=in_ring(k), device_id_type=MESH)
 
         load_ids.wait()
-        at_row = lax.broadcasted_iota(jnp.int32, (rows, IDS), 0)
-        lane = lax.broadcasted_iota(jnp.int32, (rows, IDS), 1)
-        ids = jnp.zeros((rows, IDS), jnp.int32)
-        for r in range(rows):
-            ids = jnp.where(at_row == r, ids_smem[r], ids)
-        hot = jnp.logical_or(
-            lane == lax.shift_right_logical(ids, 5), lane == HALF + jnp.bitwise_and(ids, HALF - 1)
-        )
-        key_slot(mine)[:, width:] = jnp.where(hot, 1.0, 0.0).astype(jnp.bfloat16)
+        lane = lax.broadcasted_iota(jnp.int32, (1, LANES), 1)
+        for at, place in ((0, lax.rem(chip, LANES // rows)), (1, z)):
+            line = jnp.zeros((1, LANES), jnp.int32)
+            for r in range(rows):
+                line = jnp.where(lane == place * rows + r, ids_smem[r], line)
+            ids_mine[at] = line
+        ids_plane[pl.ds(chip, 1)] = ids_mine[0:1]
+        ids_ring[pl.ds(z, 1)] = ids_mine[1:2]
         load.wait()
-        query_slot(z)[...] = key_slot(mine)[...]
+        query_slot(z)[...] = key_slot(0, chip)[...]
         pl.semaphore_wait(barrier, plane - 1 + nz - 1)
 
+    def query_via(k):
+        if min(k, nz - k) < 3:
+            return 0
+        return 2 if k <= nz // 2 else nz - 2
+
     def query_copy(k):
-        return pltpu.make_async_remote_copy(
-            src_ref=key_slot(mine),
-            dst_ref=query_slot(z),
+        via = query_via(k)
+        source = (z + nz - via) % nz
+        return pltpu.make_async_remote_copy(
+            src_ref=query_slot(source) if via else key_slot(0, chip),
+            dst_ref=query_slot(source),
             send_sem=query_send.at[k],
             recv_sem=query_recv.at[k],
+            device_id=in_ring((k + nz - via) % nz),
+            device_id_type=MESH,
+        )
+
+    def key_via(offset):
+        dy, dx = offset
+        if dy == 0 or dx == 0:
+            return (0, 0)
+        if min(dy, ny - dy) == min(dx, nx - dx):
+            return (dy, 0) if dy == dx else (0, dx)
+        return (dy, 0) if min(dy, ny - dy) == 2 else (0, dx)
+
+    def key_copy(offset):
+        at = offset[0] * nx + offset[1]
+        via = key_via(offset)
+        source = (y + ny - via[0]) % ny * nx + (x + nx - via[1]) % nx
+        onward = ((offset[0] + ny - via[0]) % ny, (offset[1] + nx - via[1]) % nx)
+        return pltpu.make_async_remote_copy(
+            src_ref=key_slot(0, source),
+            dst_ref=key_slot(0, source),
+            send_sem=key_send.at[at],
+            recv_sem=key_recv.at[at],
+            device_id=in_plane((*onward, 0)),
+            device_id_type=MESH,
+        )
+
+    def passed_on(offset):
+        at = offset[0] * nx + offset[1]
+        came_from = (y + ny - offset[0]) % ny * nx + (x + nx - offset[1]) % nx
+        return pltpu.make_async_remote_copy(
+            src_ref=key_slot(0, came_from),
+            dst_ref=key_slot(1, came_from),
+            send_sem=fwd_send.at[at],
+            recv_sem=fwd_recv.at[at],
+            device_id=sibling,
+            device_id_type=MESH,
+        )
+
+    def ids_plane_copy(offset):
+        return pltpu.make_async_remote_copy(
+            src_ref=ids_mine.at[0],
+            dst_ref=ids_plane.at[offset[2] * chips + chip],
+            send_sem=ids_plane_sem.at[0],
+            recv_sem=ids_plane_sem.at[1],
+            device_id=in_plane(offset),
+            device_id_type=MESH,
+        )
+
+    def ids_ring_copy(k):
+        return pltpu.make_async_remote_copy(
+            src_ref=ids_mine.at[1],
+            dst_ref=ids_ring.at[z],
+            send_sem=ids_ring_sem.at[0],
+            recv_sem=ids_ring_sem.at[1],
             device_id=in_ring(k),
             device_id_type=MESH,
         )
 
-    def key_copy(offset):
-        return pltpu.make_async_remote_copy(
-            src_ref=key_slot(mine),
-            dst_ref=key_slot(mine),
-            send_sem=key_send.at[offset[0] * nx + offset[1]],
-            recv_sem=key_recv.at[offset[0] * nx + offset[1]],
-            device_id=in_plane((*offset, 0)),
-            device_id_type=MESH,
-        )
-
-    def passed_on(offset):
-        came_from = (y + ny - offset[0]) % ny * nx + (x + nx - offset[1]) % nx
-        slot = key_slot(came_from * nc + c)
-        return pltpu.make_async_remote_copy(
-            src_ref=slot,
-            dst_ref=slot,
-            send_sem=fwd_send.at[offset[0] * nx + offset[1]],
-            recv_sem=fwd_recv.at[offset[0] * nx + offset[1]],
-            device_id=sibling,
-            device_id_type=MESH,
-        )
+    query_direct = [k for k in ring if not query_via(k)]
+    query_relays = [k for k in ring if query_via(k)]
+    key_direct = [o for o in chips_away if not any(key_via(o))]
+    key_direct.sort(key=lambda o: 0 if 2 in o else 1 if 0 not in o else 2)
+    key_relays = [o for o in chips_away if any(key_via(o))]
 
     with jax.named_scope("gather_start"):
-        query_copy(ring[0]).start()
-        for offset in chips_away[:5]:
+        for offset in key_direct[:2]:
             key_copy(offset).start()
-        for k in ring[1:]:
+        for k in query_direct[:2]:
             query_copy(k).start()
-        for offset in chips_away[5:]:
+        for offset in key_direct[2:]:
             key_copy(offset).start()
+        for k in query_direct[2:]:
+            query_copy(k).start()
         passed_on((0, 0)).start()
+        for offset in others:
+            ids_plane_copy(offset).start()
+        for k in ring:
+            ids_ring_copy(k).start()
+
+    with jax.named_scope("gather_relay"):
+        for offset in key_direct[2:] + key_direct[:2]:
+            key_copy(offset).wait_recv()
+            for further in key_relays:
+                if key_via(further) == offset:
+                    key_copy(further).start()
+            passed_on(offset).start()
+        for k in query_direct[:2]:
+            query_copy(k).wait_recv()
+            for further in query_relays:
+                if query_via(further) == k:
+                    query_copy(further).start()
 
     with jax.named_scope("key_pass_on"):
-        for offset in chips_away[::-1]:
+        for offset in key_relays[::-1]:
             key_copy(offset).wait_recv()
             passed_on(offset).start()
 
-    with jax.named_scope("gather_wait"):
-        for k in ring[::-1]:
+    with jax.named_scope("query_wait"):
+        for k in query_direct[2:] + query_relays:
             query_copy(k).wait_recv()
+
+    def scores_with(half):
+        return lax.dot_general(
+            queries[...],
+            keys[half * n_half : (half + 1) * n_half],
+            (((1,), (1,)), ((), ())),
+            preferred_element_type=jnp.float32,
+        ) * (1.0 / width**0.5)
+
+    def down_log_sum_exp(values):
+        peak = jnp.max(values, axis=0, keepdims=True)
+        return peak + jnp.log(jnp.sum(jnp.exp(values - peak), axis=0, keepdims=True))
+
+    with jax.named_scope("own_scores"):
+        scores_own = scores_with(0)
+        q_at = lax.broadcasted_iota(jnp.int32, (n_query, n_half), 0)
+        k_at = lax.broadcasted_iota(jnp.int32, (n_query, n_half), 1)
+        selfs = jnp.logical_and(k_at - q_at == rows * (chip - z), q_at // rows == z)
+        masked_own = jnp.where(selfs, jnp.float32(-1e30), scores_own)
+        lse_own = down_log_sum_exp(masked_own)
+
+    with jax.named_scope("passed_wait"):
         for offset in [(0, 0)] + chips_away[::-1]:
             passed_on(offset).wait_recv()
 
-    contract_last = (((1,), (1,)), ((), ()))
     with jax.named_scope("scores"):
-        scores = lax.dot_general(
-            queries[:, :width], keys[:, :width], contract_last, preferred_element_type=jnp.float32
-        ) * (1.0 / width**0.5)
-        same = (
-            lax.dot_general(
-                queries[:, width:],
-                keys[:, width:],
-                contract_last,
-                preferred_element_type=jnp.float32,
-            )
-            > 1.5
-        )
-        q_at = lax.broadcasted_iota(jnp.int32, (n_query, n_key), 0)
-        k_at = lax.broadcasted_iota(jnp.int32, (n_query, n_key), 1)
-        selfs = jnp.logical_and(k_at - q_at == rows * (mine - z), q_at // rows == z)
-        positive = jnp.logical_and(same, jnp.logical_not(selfs))
-        pos = jnp.where(positive, 1.0, 0.0)
-        masked = jnp.where(selfs, jnp.float32(-1e30), scores)
+        scores_other = scores_with(1)
+        masked = jnp.concatenate([masked_own, scores_other], axis=1)
+        col_lse = jnp.concatenate([lse_own, down_log_sum_exp(scores_other)], axis=1)
+
+    with jax.named_scope("positives"):
+        wait_bytes(ids_plane.at[pl.ds(0, plane - 1)], ids_plane_sem.at[1])
+        wait_bytes(ids_ring.at[pl.ds(0, nz - 1)], ids_ring_sem.at[1])
+        query_ids = jnp.sum(ids_ring[...], axis=0)
+        tall_ids = jnp.transpose(jnp.broadcast_to(query_ids, (LANES, n_query)))
+        group = LANES // rows
+        same = [
+            tall_ids == jnp.sum(ids_plane[at : at + group], axis=0)
+            for at in range(0, plane, group)
+        ]
+        same = jnp.concatenate([jnp.where(one, 1.0, 0.0) for one in same], axis=1)
+        pos = jnp.concatenate(
+            [jnp.where(selfs, 0.0, same[:, :n_half]), same[:, n_half:]], axis=1
+        )
 
     with jax.named_scope("stats"):
-        peak = jnp.max(masked, axis=0, keepdims=True)
-        col_lse = peak + jnp.log(jnp.sum(jnp.exp(masked - peak), axis=0, keepdims=True))
         col_count = jnp.sum(pos, axis=0, keepdims=True)
-        for r in range(n_key // LANES):
+        blocks = n_key // LANES
+        for r in range(blocks):
             at = slice(r * LANES, (r + 1) * LANES)
-            col_mine[0, r : r + 1, :] = col_lse[:, at]
-            col_mine[1, r : r + 1, :] = col_count[:, at]
-        col_all[pl.ds(mine, 1)] = col_mine[...][None]
+            for turn in range(2):
+                to = (r + turn * blocks // 2) % blocks
+                col_mine[turn, 0, to : to + 1, :] = col_lse[:, at]
+                col_mine[turn, 1, to : to + 1, :] = col_count[:, at]
+        col_all[pl.ds(chip, 1)] = col_mine[0:1]
 
     def col_copy(offset):
         return pltpu.make_async_remote_copy(
-            src_ref=col_mine,
-            dst_ref=col_all.at[mine],
+            src_ref=col_mine.at[offset[2]],
+            dst_ref=col_all.at[offset[2] * chips + chip],
             send_sem=col_sem.at[0],
             recv_sem=col_sem.at[1],
             device_id=in_plane(offset),
@@ -216,7 +303,7 @@
     with jax.named_scope("row_stats"):
         peak = jnp.max(masked, axis=1, keepdims=True)
         row_lse = peak + jnp.log(jnp.sum(jnp.exp(masked - peak), axis=1, keepdims=True))
-        row_possum = jnp.sum(pos * scores, axis=1, keepdims=True)
+        row_possum = jnp.sum(pos * masked, axis=1, keepdims=True)
         row_count = jnp.sum(pos, axis=1, keepdims=True)
         lane = lax.broadcasted_iota(jnp.int32, (n_query, LANES), 1)
         tall = jnp.where(lane == 0, row_lse, jnp.where(lane == 1, row_possum, row_count))
@@ -249,10 +336,8 @@
         mirrored = (jnp.exp(masked - flat_lse) - pos * flat_inverse) * (1.0 / whole)
 
     with jax.named_scope("gradient"):
-        both = jnp.concatenate([weight.astype(jnp.bfloat16), mirrored.astype(jnp.bfloat16)], axis=0)
-        terms = jnp.dot(both, keys[:, :width], preferred_element_type=jnp.float32)
-        terms = (terms[:n_query] + terms[n_query:]) * (1.0 / width**0.5)
-        part_mine[...] = terms.astype(jnp.bfloat16)
+        weight = weight.astype(jnp.bfloat16)
+        mirrored = mirrored.astype(jnp.bfloat16)
 
     def part_copy(to):
         return pltpu.make_async_remote_copy(
@@ -267,7 +352,7 @@
     def loss_copy(offset):
         return pltpu.make_async_remote_copy(
             src_ref=loss_mine,
-            dst_ref=loss_all.at[mine],
+            dst_ref=loss_all.at[offset[2] * chips + chip],
             send_sem=loss_sem.at[0],
             recv_sem=loss_sem.at[1],
             device_id=in_plane(offset),
@@ -275,17 +360,24 @@
         )
 
     with jax.named_scope("reduce_start"):
-        for to in range(nz):
-
-            @pl.when(z != to)
-            def _():
-                part_copy(to).start()
+        some = n_query // 2
+        for first in range(0, n_query, some):
+            last = first + some
+            both = jnp.concatenate([weight[first:last], mirrored[first:last]], axis=0)
+            terms = jnp.dot(both, keys[...], preferred_element_type=jnp.float32)
+            terms = (terms[:some] + terms[some:]) * (1.0 / width**0.5)
+            part_mine[first:last] = terms.astype(jnp.bfloat16)
+            for to in range(first // rows, last // rows):
+
+                @pl.when(z != to)
+                def _():
+                    part_copy(to).start()
 
         part_all[pl.ds(z, 1)] = part_mine[pl.ds(pl.multiple_of(z * rows, rows), rows), :][None]
 
     with jax.named_scope("loss_start"):
         loss_mine[...] = query_lse - query_possum * query_inverse
-        loss_all[pl.ds(mine, 1)] = loss_mine[...][None]
+        loss_all[pl.ds(chip, 1)] = loss_mine[...][None]
         for offset in others:
             loss_copy(offset).start()
 
@@ -296,6 +388,8 @@
             key_copy(offset).wait_send()
         for offset in [(0, 0)] + chips_away:
             passed_on(offset).wait_send()
+        wait_bytes(ids_plane.at[pl.ds(0, plane - 1)], ids_plane_sem.at[0])
+        wait_bytes(ids_ring.at[pl.ds(0, nz - 1)], ids_ring_sem.at[0])
 
     with jax.named_scope("stats_sent"):
         wait_bytes(col_all.at[pl.ds(0, plane - 1)], col_sem.at[0])
@@ -336,10 +430,13 @@
             pl.BlockSpec(memory_space=pltpu.VMEM),
         ),
         scratch_shapes=[
-            pltpu.VMEM((n_key, width + IDS), jnp.bfloat16),
-            pltpu.VMEM((n_query, width + IDS), jnp.bfloat16),
+            pltpu.VMEM((n_key, width), jnp.bfloat16),
+            pltpu.VMEM((n_query, width), jnp.bfloat16),
             pltpu.SMEM((rows,), jnp.int32),
-            pltpu.VMEM((2, n_key // LANES, LANES), jnp.float32),
+            pltpu.VMEM((2, 1, LANES), jnp.int32),
+            pltpu.VMEM((plane, 1, LANES), jnp.int32),
+            pltpu.VMEM((nz, 1, LANES), jnp.int32),
+            pltpu.VMEM((2, 2, n_key // LANES, LANES), jnp.float32),
             pltpu.VMEM((plane, 2, n_key // LANES, LANES), jnp.float32),
             pltpu.VMEM((4, n_query), jnp.float32),
             pltpu.VMEM((nz, 4, n_query), jnp.float32),
@@ -354,6 +451,8 @@
             dma((chips,)),
             dma((nz,)),
             dma((nz,)),
+            dma((2,)),
+            dma((2,)),
             dma((2,)),
             dma((2,)),
             dma((2,)),

time: 36 us -> 34.6 us (0.961)
  Pallas kernels: 35.2 us -> 33.5 us
    pallas_call x1, Pallas kernels: 34.6 us -> 32.9 us  [on_device(): pl.pallas_call(functools.partial(kernel, (ny, nz, nx, nc, rows, width)),...]
where the time goes in v3:
time: 34.6 us; the launch traced here: 34.1 us
  Pallas kernels  33.5 us (97%)
  between operations  0.64 us (2%)
    pallas_call x1, Pallas kernels, on_device(): pl.pallas_call(functools.partial(kernel, (ny, nz, nx, nc, rows, width)),...  32.9 us

profile of v3, /device:TPU:32, one launch (start us, length us, event | category | flops | bytes accessed | tf_op | source)
XLA Modules:
  0.0 34.1 jit_solution(4957678787152284167)
XLA Ops:
  0.6 32.9 %shard_map.41 = (f32[8,128]{1,0:T(8,128)S(1)}, bf16[16,1024]{1,0:T(8,128)(2,1)S(1)}) custom-call(bf16[16,1024]{1,0:T(8,128)(2,1)} %emb_ref.1, s32[16]{0:T(128)} %ids_ref.1), custom_call_target="tpu_custom_call" | custom-call | tf_op jit(solution)/shard_map/pallas_call | solution.py:421
  33.5 0.6 %shard_map.42 = (f32[1,1]{1,0:T(1,128)}, bf16[16,1024]{1,0:T(8,128)(2,1)}) custom-call(f32[8,128]{1,0:T(8,128)S(1)} %get-tuple-element.6.loss_in, bf16[16,1024]{1,0:T(8,128)(2,1)S(1)} %get-tuple-element.7.grad_in), custom_call_target="tpu_custom_call" | custom-call | tf_op jit(solution)/shard_map/pallas_call | solution.py:470

commit v4 on v3

--- a/solution.py
+++ b/solution.py
@@ -11,6 +11,8 @@
 MESH = pl.DeviceIdType.MESH
 ALL = ("y", "z", "x", "c")
 LANES = 128
+IDS = 128
+HALF = 32
 
 
 def wait_bytes(ref, sem):
@@ -26,9 +28,6 @@
     keys,
     queries,
     ids_smem,
-    ids_mine,
-    ids_plane,
-    ids_ring,
     col_mine,
     col_all,
     row_mine,
@@ -44,8 +43,6 @@
     fwd_recv,
     query_send,
     query_recv,
-    ids_plane_sem,
-    ids_ring_sem,
     col_sem,
     row_sem,
     part_sem,
@@ -76,53 +73,10 @@
         start = half * n_half + pl.multiple_of(k * rows, rows)
         return keys.at[pl.ds(start, rows)]
 
-    def query_slot(k):
-        return queries.at[pl.ds(pl.multiple_of(k * rows, rows), rows)]
-
-    load = pltpu.make_async_copy(emb_ref, key_slot(0, chip), in_sem.at[0])
-    load.start()
-    load_ids = pltpu.make_async_copy(ids_ref, ids_smem, in_sem.at[1])
-    load_ids.start()
-
-    with jax.named_scope("barrier"):
-        barrier = pltpu.get_barrier_semaphore()
-
-        for k in ring[:1]:
-            pl.semaphore_signal(barrier, inc=1, device_id=in_ring(k), device_id_type=MESH)
-        for offset in others:
-            pl.semaphore_signal(barrier, inc=1, device_id=in_plane(offset), device_id_type=MESH)
-        for k in ring[1:]:
-            pl.semaphore_signal(barrier, inc=1, device_id=in_ring(k), device_id_type=MESH)
-
-        load_ids.wait()
-        lane = lax.broadcasted_iota(jnp.int32, (1, LANES), 1)
-        for at, place in ((0, lax.rem(chip, LANES // rows)), (1, z)):
-            line = jnp.zeros((1, LANES), jnp.int32)
-            for r in range(rows):
-                line = jnp.where(lane == place * rows + r, ids_smem[r], line)
-            ids_mine[at] = line
-        ids_plane[pl.ds(chip, 1)] = ids_mine[0:1]
-        ids_ring[pl.ds(z, 1)] = ids_mine[1:2]
-        load.wait()
-        query_slot(z)[...] = key_slot(0, chip)[...]
-        pl.semaphore_wait(barrier, plane - 1 + nz - 1)
-
     def query_via(k):
         if min(k, nz - k) < 3:
             return 0
         return 2 if k <= nz // 2 else nz - 2
-
-    def query_copy(k):
-        via = query_via(k)
-        source = (z + nz - via) % nz
-        return pltpu.make_async_remote_copy(
-            src_ref=query_slot(source) if via else key_slot(0, chip),
-            dst_ref=query_slot(source),
-            send_sem=query_send.at[k],
-            recv_sem=query_recv.at[k],
-            device_id=in_ring((k + nz - via) % nz),
-            device_id_type=MESH,
-        )
 
     def key_via(offset):
         dy, dx = offset
@@ -132,6 +86,57 @@
             return (dy, 0) if dy == dx else (0, dx)
         return (dy, 0) if min(dy, ny - dy) == 2 else (0, dx)
 
+    query_direct = [k for k in ring if not query_via(k)]
+    query_relays = [k for k in ring if query_via(k)]
+    key_direct = [o for o in chips_away if not any(key_via(o))]
+    key_direct.sort(key=lambda o: 0 if 2 in o else 1 if 0 not in o else 2)
+    key_relays = [o for o in chips_away if any(key_via(o))]
+
+    def query_slot(k):
+        return queries.at[pl.ds(pl.multiple_of(k * rows, rows), rows)]
+
+    load = pltpu.make_async_copy(emb_ref, key_slot(0, chip).at[:, pl.ds(0, width)], in_sem.at[0])
+    load.start()
+    load_ids = pltpu.make_async_copy(ids_ref, ids_smem, in_sem.at[1])
+    load_ids.start()
+
+    with jax.named_scope("barrier"):
+        barrier = pltpu.get_barrier_semaphore()
+
+        for offset in key_direct:
+            pl.semaphore_signal(
+                barrier, inc=1, device_id=in_plane((*offset, 0)), device_id_type=MESH
+            )
+        for k in query_direct:
+            pl.semaphore_signal(barrier, inc=1, device_id=in_ring(k), device_id_type=MESH)
+        pl.semaphore_signal(barrier, inc=1, device_id=sibling, device_id_type=MESH)
+
+        load_ids.wait()
+        at_row = lax.broadcasted_iota(jnp.int32, (rows, IDS), 0)
+        lane = lax.broadcasted_iota(jnp.int32, (rows, IDS), 1)
+        ids = jnp.zeros((rows, IDS), jnp.int32)
+        for r in range(rows):
+            ids = jnp.where(at_row == r, ids_smem[r], ids)
+        hot = jnp.logical_or(
+            lane == lax.shift_right_logical(ids, 5), lane == HALF + jnp.bitwise_and(ids, HALF - 1)
+        )
+        key_slot(0, chip)[:, width:] = jnp.where(hot, 1.0, 0.0).astype(jnp.bfloat16)
+        load.wait()
+        query_slot(z)[...] = key_slot(0, chip)[...]
+        pl.semaphore_wait(barrier, len(key_direct) + len(query_direct) + 1)
+
+    def query_copy(k):
+        via = query_via(k)
+        source = (z + nz - via) % nz
+        return pltpu.make_async_remote_copy(
+            src_ref=query_slot(source) if via else key_slot(0, chip),
+            dst_ref=query_slot(source),
+            send_sem=query_send.at[k],
+            recv_sem=query_recv.at[k],
+            device_id=in_ring((k + nz - via) % nz),
+            device_id_type=MESH,
+        )
+
     def key_copy(offset):
         at = offset[0] * nx + offset[1]
         via = key_via(offset)
@@ -157,32 +162,6 @@
             device_id=sibling,
             device_id_type=MESH,
         )
-
-    def ids_plane_copy(offset):
-        return pltpu.make_async_remote_copy(
-            src_ref=ids_mine.at[0],
-            dst_ref=ids_plane.at[offset[2] * chips + chip],
-            send_sem=ids_plane_sem.at[0],
-            recv_sem=ids_plane_sem.at[1],
-            device_id=in_plane(offset),
-            device_id_type=MESH,
-        )
-
-    def ids_ring_copy(k):
-        return pltpu.make_async_remote_copy(
-            src_ref=ids_mine.at[1],
-            dst_ref=ids_ring.at[z],
-            send_sem=ids_ring_sem.at[0],
-            recv_sem=ids_ring_sem.at[1],
-            device_id=in_ring(k),
-            device_id_type=MESH,
-        )
-
-    query_direct = [k for k in ring if not query_via(k)]
-    query_relays = [k for k in ring if query_via(k)]
-    key_direct = [o for o in chips_away if not any(key_via(o))]
-    key_direct.sort(key=lambda o: 0 if 2 in o else 1 if 0 not in o else 2)
-    key_relays = [o for o in chips_away if any(key_via(o))]
 
     with jax.named_scope("gather_start"):
         for offset in key_direct[:2]:
@@ -194,10 +173,6 @@
         for k in query_direct[2:]:
             query_copy(k).start()
         passed_on((0, 0)).start()
-        for offset in others:
-            ids_plane_copy(offset).start()
-        for k in ring:
-            ids_ring_copy(k).start()
 
     with jax.named_scope("gather_relay"):
         for offset in key_direct[2:] + key_direct[:2]:
@@ -223,8 +198,8 @@
 
     def scores_with(half):
         return lax.dot_general(
-            queries[...],
-            keys[half * n_half : (half + 1) * n_half],
+            queries[:, :width],
+            keys[half * n_half : (half + 1) * n_half, :width],
             (((1,), (1,)), ((), ())),
             preferred_element_type=jnp.float32,
         ) * (1.0 / width**0.5)
@@ -251,16 +226,13 @@
         col_lse = jnp.concatenate([lse_own, down_log_sum_exp(scores_other)], axis=1)
 
     with jax.named_scope("positives"):
-        wait_bytes(ids_plane.at[pl.ds(0, plane - 1)], ids_plane_sem.at[1])
-        wait_bytes(ids_ring.at[pl.ds(0, nz - 1)], ids_ring_sem.at[1])
-        query_ids = jnp.sum(ids_ring[...], axis=0)
-        tall_ids = jnp.transpose(jnp.broadcast_to(query_ids, (LANES, n_query)))
-        group = LANES // rows
-        same = [
-            tall_ids == jnp.sum(ids_plane[at : at + group], axis=0)
-            for at in range(0, plane, group)
-        ]
-        same = jnp.concatenate([jnp.where(one, 1.0, 0.0) for one in same], axis=1)
+        same = lax.dot_general(
+            queries[:, width:],
+            keys[:, width:],
+            (((1,), (1,)), ((), ())),
+            preferred_element_type=jnp.float32,
+        )
+        same = jnp.where(same > 1.5, 1.0, 0.0)
         pos = jnp.concatenate(
             [jnp.where(selfs, 0.0, same[:, :n_half]), same[:, n_half:]], axis=1
         )
@@ -364,7 +336,7 @@
         for first in range(0, n_query, some):
             last = first + some
             both = jnp.concatenate([weight[first:last], mirrored[first:last]], axis=0)
-            terms = jnp.dot(both, keys[...], preferred_element_type=jnp.float32)
+            terms = jnp.dot(both, keys[:, :width], preferred_element_type=jnp.float32)
             terms = (terms[:some] + terms[some:]) * (1.0 / width**0.5)
             part_mine[first:last] = terms.astype(jnp.bfloat16)
             for to in range(first // rows, last // rows):
@@ -388,8 +360,6 @@
             key_copy(offset).wait_send()
         for offset in [(0, 0)] + chips_away:
             passed_on(offset).wait_send()
-        wait_bytes(ids_plane.at[pl.ds(0, plane - 1)], ids_plane_sem.at[0])
-        wait_bytes(ids_ring.at[pl.ds(0, nz - 1)], ids_ring_sem.at[0])
 
     with jax.named_scope("stats_sent"):
         wait_bytes(col_all.at[pl.ds(0, plane - 1)], col_sem.at[0])
@@ -430,12 +400,9 @@
             pl.BlockSpec(memory_space=pltpu.VMEM),
         ),
         scratch_shapes=[
-            pltpu.VMEM((n_key, width), jnp.bfloat16),
-            pltpu.VMEM((n_query, width), jnp.bfloat16),
+            pltpu.VMEM((n_key, width + IDS), jnp.bfloat16),
+            pltpu.VMEM((n_query, width + IDS), jnp.bfloat16),
             pltpu.SMEM((rows,), jnp.int32),
-            pltpu.VMEM((2, 1, LANES), jnp.int32),
-            pltpu.VMEM((plane, 1, LANES), jnp.int32),
-            pltpu.VMEM((nz, 1, LANES), jnp.int32),
             pltpu.VMEM((2, 2, n_key // LANES, LANES), jnp.float32),
             pltpu.VMEM((plane, 2, n_key // LANES, LANES), jnp.float32),
             pltpu.VMEM((4, n_query), jnp.float32),
@@ -455,8 +422,6 @@
             dma((2,)),
             dma((2,)),
             dma((2,)),
-            dma((2,)),
-            dma((2,)),
         ],
         compiler_params=pltpu.CompilerParams(
             collective_id=0, has_side_effects=True, vmem_limit_bytes=60 * 1024 * 1024

time: 34.6 us -> 33.3 us (0.962)
  Pallas kernels: 33.5 us -> 32.1 us
    pallas_call x1, Pallas kernels: 32.9 us -> 31.5 us  [on_device(): pl.pallas_call(functools.partial(kernel, (ny, nz, nx, nc, rows, width)),...]
where the time goes in v4:
time: 33.3 us; the launch traced here: 32.8 us
  Pallas kernels  32.1 us (96%)
  between operations  0.64 us (2%)
    pallas_call x1, Pallas kernels, on_device(): pl.pallas_call(functools.partial(kernel, (ny, nz, nx, nc, rows, width)),...  31.5 us

profile of v4, /device:TPU:32, one launch (start us, length us, event | category | flops | bytes accessed | tf_op | source)
XLA Modules:
  0.0 32.8 jit_solution(9659573105806091653)
XLA Ops:
  0.6 31.5 %shard_map.41 = (f32[8,128]{1,0:T(8,128)S(1)}, bf16[16,1024]{1,0:T(8,128)(2,1)S(1)}) custom-call(bf16[16,1024]{1,0:T(8,128)(2,1)} %emb_ref.1, s32[16]{0:T(128)} %ids_ref.1), custom_call_target="tpu_custom_call" | custom-call | tf_op jit(solution)/shard_map/pallas_call | solution.py:391
  32.2 0.6 %shard_map.42 = (f32[1,1]{1,0:T(1,128)}, bf16[16,1024]{1,0:T(8,128)(2,1)}) custom-call(f32[8,128]{1,0:T(8,128)S(1)} %get-tuple-element.6.loss_in, bf16[16,1024]{1,0:T(8,128)(2,1)S(1)} %get-tuple-element.7.grad_in), custom_call_target="tpu_custom_call" | custom-call | tf_op jit(solution)/shard_map/pallas_call | solution.py:435

commit v5 on v4

--- a/solution.py
+++ b/solution.py
@@ -151,28 +151,24 @@
             device_id_type=MESH,
         )
 
-    def passed_on(offset):
-        at = offset[0] * nx + offset[1]
-        came_from = (y + ny - offset[0]) % ny * nx + (x + nx - offset[1]) % nx
-        return pltpu.make_async_remote_copy(
-            src_ref=key_slot(0, came_from),
-            dst_ref=key_slot(1, came_from),
-            send_sem=fwd_send.at[at],
-            recv_sem=fwd_recv.at[at],
+    lines = sorted(range(ny), key=lambda dy: min(dy, ny - dy))
+
+    def passed_on(dy):
+        line = pl.multiple_of((y + ny - dy) % ny * nx * rows, nx * rows)
+        return pltpu.make_async_remote_copy(
+            src_ref=keys.at[pl.ds(line, nx * rows)],
+            dst_ref=keys.at[pl.ds(n_half + line, nx * rows)],
+            send_sem=fwd_send.at[dy],
+            recv_sem=fwd_recv.at[dy],
             device_id=sibling,
             device_id_type=MESH,
         )
 
     with jax.named_scope("gather_start"):
-        for offset in key_direct[:2]:
+        for k in query_direct:
+            query_copy(k).start()
+        for offset in key_direct:
             key_copy(offset).start()
-        for k in query_direct[:2]:
-            query_copy(k).start()
-        for offset in key_direct[2:]:
-            key_copy(offset).start()
-        for k in query_direct[2:]:
-            query_copy(k).start()
-        passed_on((0, 0)).start()
 
     with jax.named_scope("gather_relay"):
         for offset in key_direct[2:] + key_direct[:2]:
@@ -180,7 +176,7 @@
             for further in key_relays:
                 if key_via(further) == offset:
                     key_copy(further).start()
-            passed_on(offset).start()
+        passed_on(0).start()
         for k in query_direct[:2]:
             query_copy(k).wait_recv()
             for further in query_relays:
@@ -188,9 +184,11 @@
                     query_copy(further).start()
 
     with jax.named_scope("key_pass_on"):
-        for offset in key_relays[::-1]:
-            key_copy(offset).wait_recv()
-            passed_on(offset).start()
+        for dy in lines[1:]:
+            for offset in key_relays[::-1]:
+                if offset[0] == dy:
+                    key_copy(offset).wait_recv()
+            passed_on(dy).start()
 
     with jax.named_scope("query_wait"):
         for k in query_direct[2:] + query_relays:
@@ -217,8 +215,8 @@
         lse_own = down_log_sum_exp(masked_own)
 
     with jax.named_scope("passed_wait"):
-        for offset in [(0, 0)] + chips_away[::-1]:
-            passed_on(offset).wait_recv()
+        for dy in lines:
+            passed_on(dy).wait_recv()
 
     with jax.named_scope("scores"):
         scores_other = scores_with(1)
@@ -268,21 +266,27 @@
             device_id_type=MESH,
         )
 
+    far = [o for o in others if min(o[0], ny - o[0]) + min(o[1], nx - o[1]) > 2]
+
     with jax.named_scope("col_start"):
-        for offset in others:
+        for offset in far:
             col_copy(offset).start()
 
     with jax.named_scope("row_stats"):
-        peak = jnp.max(masked, axis=1, keepdims=True)
-        row_lse = peak + jnp.log(jnp.sum(jnp.exp(masked - peak), axis=1, keepdims=True))
+        row_peak = jnp.max(masked, axis=1, keepdims=True)
+        row_exps = jnp.exp(masked - row_peak)
+        row_lse = row_peak + jnp.log(jnp.sum(row_exps, axis=1, keepdims=True))
         row_possum = jnp.sum(pos * masked, axis=1, keepdims=True)
         row_count = jnp.sum(pos, axis=1, keepdims=True)
         lane = lax.broadcasted_iota(jnp.int32, (n_query, LANES), 1)
         tall = jnp.where(lane == 0, row_lse, jnp.where(lane == 1, row_possum, row_count))
         row_mine[...] = jnp.transpose(tall)[:4]
-        row_all[pl.ds(z, 1)] = row_mine[...][None]
         for k in ring:
             row_copy(k).start()
+        for offset in others:
+            if offset not in far:
+                col_copy(offset).start()
+        row_all[pl.ds(z, 1)] = row_mine[...][None]
 
     with jax.named_scope("stats_wait"):
         wait_bytes(col_all.at[pl.ds(0, plane - 1)], col_sem.at[1])
@@ -358,8 +362,8 @@
             query_copy(k).wait_send()
         for offset in chips_away:
             key_copy(offset).wait_send()
-        for offset in [(0, 0)] + chips_away:
-            passed_on(offset).wait_send()
+        for dy in lines:
+            passed_on(dy).wait_send()
 
     with jax.named_scope("stats_sent"):
         wait_bytes(col_all.at[pl.ds(0, plane - 1)], col_sem.at[0])

time: 33.3 us -> 33.2 us (level)
  no operation moved by 1% of the time
where the time goes in v5:
time: 33.2 us; the launch traced here: 32.7 us
  Pallas kernels  32.1 us (97%)
  between operations  0.64 us (2%)
    pallas_call x1, Pallas kernels, on_device(): pl.pallas_call(functools.partial(kernel, (ny, nz, nx, nc, rows, width)),...  31.5 us

profile of v5, /device:TPU:32, one launch (start us, length us, event | category | flops | bytes accessed | tf_op | source)
XLA Modules:
  0.0 32.7 jit_solution(13802852260323521952)
XLA Ops:
  0.6 31.5 %shard_map.41 = (f32[8,128]{1,0:T(8,128)S(1)}, bf16[16,1024]{1,0:T(8,128)(2,1)S(1)}) custom-call(bf16[16,1024]{1,0:T(8,128)(2,1)} %emb_ref.1, s32[16]{0:T(128)} %ids_ref.1), custom_call_target="tpu_custom_call" | custom-call | tf_op jit(solution)/shard_map/pallas_call | solution.py:395
  32.1 0.6 %shard_map.42 = (f32[1,1]{1,0:T(1,128)}, bf16[16,1024]{1,0:T(8,128)(2,1)}) custom-call(f32[8,128]{1,0:T(8,128)S(1)} %get-tuple-element.6.loss_in, bf16[16,1024]{1,0:T(8,128)(2,1)S(1)} %get-tuple-element.7.grad_in), custom_call_target="tpu_custom_call" | custom-call | tf_op jit(solution)/shard_map/pallas_call | solution.py:439
